TPU v7x, 256 devices: a whole 4x4x8 slice. The times are simulated.
256 devices in a mesh: seq: 64 (over z, x, core), rep: 4 (over y).
Axes of the slice: x: 4, y: 4, z: 8, core: 2. Of those that a mesh axis runs over, the one named last changes fastest.
Arguments:
- frames: bfloat16 [65536, 1536], P(('rep', 'seq')), parts along dimension 0, may hold values from -6 to 6
- lengths: int32 [512], P('rep'), parts along dimension 0, may hold values from 1 to 256, 16384 in all
- norm_attn: float32 [1536], replicated, may hold values from 0.25 to 1.75
- w_query: bfloat16 [1536, 768], P('seq'), may hold values from -2 to 2, as said below
- w_key: bfloat16 [1536, 768], P('seq'), may hold values from -2 to 2, as said below
- w_value: bfloat16 [1536, 768], P('seq'), may hold values from -0.15625 to 0.15625
- w_out: bfloat16 [768, 1536], P('seq'), may hold values from -0.21875 to 0.21875
- norm_conv: float32 [1536], replicated, may hold values from 0.25 to 1.75
- w_expand: bfloat16 [1536, 1536], P('seq'), may hold values from -0.15625 to 0.15625
- kernel: float32 [31, 768], replicated, may hold values from -1 to 1
- bn_gain: float32 [768], replicated, may hold values from 0.25 to 1.75
- bn_bias: float32 [768], replicated, may hold values from -3 to 3
- w_shrink: bfloat16 [768, 1536], P('seq'), may hold values from -0.21875 to 0.21875
- norm_final: float32 [1536], replicated, may hold values from 0.25 to 1.75
Outputs:
- block_out: bfloat16 [65536, 1536], P(('rep', 'seq')), parts along dimension 0
- pooled: float32 [512, 1536], P('rep'), parts along dimension 0
There are 4 independent parts, one for each index of `rep`. A program takes and returns all parts, laid end to end along the dimension named above; an argument that names none is the same for every part. Nothing has to cross between parts.
Inputs may be any that keep to these rules, and one draw needn't show every extreme that they name: The lengths of the recordings sum to 16384. `w_query`: entries of order 1536**-0.5. `w_key`: entries of order 1536**-0.5.
All inputs are finite; a program needn't handle non-finite values.
Results may differ from a plain program's by a relative error of at most 0.013.
Values may be sent and summed in bfloat16 or wider, within the bound.
A program may use at most 64 MiB of HBM per device.

v0:
```python
import jax
import jax.numpy as jnp
from jax import lax
from jax.experimental import pallas as pl
from jax.experimental.pallas import tpu as pltpu
from jax.sharding import PartitionSpec as P

H = 8
HD = 96
KERNEL = 31
HALF = 15
MESH = pl.DeviceIdType.MESH
F32 = jnp.float32
BF16 = jnp.bfloat16
NZ, NX, NY = 8, 4, 4
ROWS = 256
D = 1536
CH = 768
NREC = 128
UNIT = 1152
COLS = 7 * UNIT
GROUPS = (
    (0, 2, (7, 7, 4), ('straight', 'ring', 'ring', 'ring', 'straight')),
    (2, 4, (7, 3, 8), ('straight', 'ring', 'ring', 'ring', 'hops')),
    (4, 6, (5, 5, 8), ('ring', 'ring', 'ring', 'ring', 'straight')),
    (6, 7, (1, 0, 8), ('straight', 'ring', 'hops', 'ring', 'ring')),
)
N_COPIES = 112
PLAN = (
    "start0", "sendfr", "packrest", "bounds", "packos", "01", "start1", "00", "02", "start3", "norma",
    "normb", "01", "11", "12", "start2", "00", "32", "01", "11", "12", "21", "normx", "normy", "10", "22",
    "02", "30", "20", "00", "32", "01", "11", "21", "12", "22", "10", "20", "30", "02", "00", "32", "11",
    "21", "10", "12", "20", "02", "30", "01", "00", "32", "22", "21", "laykv", "12", "10", "mmkv0", "11",
    "20", "mmkv1", "10", "32", "sendkv", "layq", "mmq", "22", "20", "layo", "21", "att0", "att1", "att2",
    "20", "att3", "21", "32", "mmo", "normc", "22", "normd", "laye", "mme0", "mme1", "32", "mme2", "sendrim",
    "conv0", "conv1", "lays", "conv2", "mms", "fin",
)


class Place:
    def __init__(self):
        self.index = lax.axis_index("seq")
        self.z = self.index // 8
        self.x = (self.index // 2) % 4
        self.c = self.index % 2
        self.y = lax.axis_index("rep")

    def at(self, dz=0, dx=0, dc=0, dy=0):
        z = (self.z + dz + NZ) % NZ
        x = (self.x + dx + NX) % NX
        c = (self.c + dc) % 2
        y = (self.y + dy + NY) % NY
        return {"seq": z * 8 + x * 2 + c, "rep": y}

    def beside(self, step):
        return {"seq": (self.index + step + 64) % 64, "rep": self.y}

    def partners(self):
        found = [self.at(dz=k) for k in range(1, NZ)]
        found += [self.at(dx=k) for k in range(1, NX)]
        found += [self.at(dy=k) for k in range(1, NY)]
        found += [self.at(dc=1), self.beside(2 * self.c - 1)]
        return found


class Copies:
    def __init__(self, send_sem, recv_sem):
        self.send_sem, self.recv_sem = send_sem, recv_sem
        self.count = 0
        self.all = []

    def sems(self):
        self.count += 1
        return {"send_sem": self.send_sem.at[self.count - 1], "recv_sem": self.recv_sem.at[self.count - 1]}

    def send(self, src, dst, device):
        copy = pltpu.make_async_remote_copy(
            src_ref=src, dst_ref=dst, device_id=device, device_id_type=MESH, **self.sems()
        )
        copy.start()
        self.all.append(copy)
        return copy

    def finish(self):
        for copy in self.all:
            copy.wait_send()


class Batch:
    def __init__(self, copies, ref, whole, device):
        self.ref, self.sems = ref, copies.sems()
        self.total = self.make(whole, device)
        copies.all.append(self)

    def make(self, region, device):
        part = self.ref.at[region]
        return pltpu.make_async_remote_copy(
            src_ref=part, dst_ref=part, device_id=device, device_id_type=MESH, **self.sems
        )

    def push(self, region, device):
        self.make(region, device).start()

    def wait_recv(self):
        self.total.wait_recv()

    def wait_send(self):
        self.total.wait_send()


class Gather:
    def __init__(self, copies, place, ref, own):
        self.copies, self.place, self.ref, self.own = copies, place, ref, own

    def batch(self, whole):
        return Batch(self.copies, self.ref, whole, self.place.at(dc=1))

    def straight(self, axis, n, region, many, shared):
        place = self.place
        me = {"z": place.z, "x": place.x, "y": place.y}[axis]
        sent = self.batch(many(n - 1))
        for k in range(1, n):
            sent.push(region(me, None), place.at(**{"d" + axis: k}))
        yield
        sent.wait_recv()
        for k in range(1, n):
            shared.push(region((me - k + n) % n, None), place.at(dc=1))

    def hops(self, region, many, shared):
        place = self.place
        me, other = place.z, place.at(dc=1)
        block = lambda k: region((me + k + NZ) % NZ, None)
        sent = self.batch(many(4))
        for k in (1, -1, 2, -2):
            sent.push(block(0), place.at(dz=k))
        yield
        sent.wait_recv()
        sent = self.batch(many(3))
        for k in (1, -1):
            sent.push(block(-2 * k), place.at(dz=k))
        for k in (1, -1):
            half = region((me - 2 * k + NZ) % NZ, 0 if k == 1 else 1)
            if half is not None:
                sent.push(half, place.at(dz=2 * k))
        for k in (1, -1, 2, -2):
            shared.push(block(k), other)
        yield
        sent.wait_recv()
        for k in (3, -3, 4):
            shared.push(block(k), other)

    def ring(self, axis, region, many, shared):
        place = self.place
        n = {"z": NZ, "x": NX, "y": NY}[axis]
        me = {"z": place.z, "x": place.x, "y": place.y}[axis]
        up, down, other = place.at(**{"d" + axis: 1}), place.at(**{"d" + axis: -1}), place.at(dc=1)
        sent = self.batch(many(2))
        sent.push(region(me, None), up)
        sent.push(region(me, None), down)
        for step in range(1, n // 2):
            low, high = (me - step + n) % n, (me + step) % n
            last = step == n // 2 - 1
            yield
            sent.wait_recv()
            sent = self.batch(many(1 if last else 2))
            sent.push(region(low, 0 if last else None), up)
            rest = region(high, 1 if last else None)
            if rest is not None:
                sent.push(rest, down)
            shared.push(region(low, None), other)
            shared.push(region(high, None), other)
        yield
        sent.wait_recv()
        shared.push(region((me + n // 2) % n, None), other)

    def part(self, order, lo, tiles, modes, shared):
        place = self.place
        quarter = tiles // 4 if "y" in order else tiles

        def cut(k, half, count):
            start, size = 0, count * 128
            if half is not None:
                first = (count + 1) // 2 * 128
                start, size = (0, first) if half == 0 else (first, size - first)
            if "y" not in order:
                return pl.ds(lo + start, size)
            return pl.ds(pl.multiple_of(lo + k * (quarter * 128) + start, 128), size)

        done = set()
        for axis in order:

            def region(k, half, axis=axis, done=frozenset(done)):
                at = {"z": place.z, "x": place.x, "y": place.y}
                at[axis] = k
                z = slice(None) if "z" in done else at["z"]
                x = slice(None) if "x" in done else at["x"]
                if half == 1 and quarter == 1:
                    return None
                return (z, x, place.c, slice(None), cut(at["y"], half, quarter))

            def many(count, axis=axis, region=region):
                at = list(region({"z": place.z, "x": place.x, "y": place.y}[axis], None))
                if axis == "y":
                    at[4] = pl.ds(lo, count * quarter * 128)
                else:
                    at["zx".index(axis)] = pl.ds(0, count)
                return tuple(at)

            mode = modes[axis]
            if mode == "hops":
                yield from self.hops(region, many, shared)
            elif mode == "ring":
                yield from self.ring(axis, region, many, shared)
            else:
                yield from self.straight(axis, {"z": NZ, "x": NX, "y": NY}[axis], region, many, shared)
            done.add(axis)

    def start(self, group):
        place = self.place
        first, end, tiles, ways = GROUPS[group]
        lo, hi = first * UNIT, end * UNIT
        quarter = tiles[2] * 32
        mid = hi - 4 * quarter
        shared = self.batch((slice(None), slice(None), place.c, slice(None), pl.ds(lo, hi - lo)))
        spans = []
        if mid > lo:
            spans.append(pl.ds(lo, mid - lo))
        if quarter:
            spans.append(pl.ds(pl.multiple_of(mid + place.y * quarter, 128), quarter))
        for cols in spans:
            region = (place.z, place.x, place.c, slice(None), cols)
            self.ref[region] = self.own[:, cols]
            shared.push(region, place.at(dc=1))
        parts = {}
        for k, (order, count) in enumerate(zip(("xz", "zx", "zxy"), tiles)):
            if count:
                parts[k] = self.part(order, lo, count, {"x": ways[0], "y": ways[1], "z": ways[2 + k]}, shared)
                lo += count * 128
        return Group(parts, shared)


class Group:
    def __init__(self, parts, shared):
        self.parts, self.shared = parts, shared
        for part in parts.values():
            next(part)

    def step(self, k):
        if next(self.parts[k], True) is not None:
            del self.parts[k]

    def finish(self):
        if self.shared is not None:
            self.shared.wait_recv()
        self.shared = None
        return not self.parts


def fold(rows8):
    half = rows8.shape[1] // 2
    return jnp.concatenate([rows8[:, :half], rows8[:, half:]], axis=0)


def pack_own(own_ref, unit, value, first):
    main = jnp.where(first, value[:16], value[8:])
    rest = jnp.where(first, value[16:], value[:8])
    whole = jnp.concatenate([main, fold(rest)], axis=1).astype(BF16)
    own_ref[:, unit * UNIT : (unit + 1) * UNIT] = whole


def unfold(low, high):
    low, high = low.astype(F32), high.astype(F32)
    left = jnp.concatenate([low[:8], high[:8]], axis=0)
    right = jnp.concatenate([low[8:], high[8:]], axis=0)
    return jnp.concatenate([left, right], axis=1).astype(BF16)


def lay_rows(g_ref, unit, w_ref, column):
    lo = unit * UNIT

    @pl.loop(0, NZ)
    def _(z):
        for x in range(NX):
            row = z * 192 + x * 48
            low, high = g_ref[z, x, 0, :, lo : lo + UNIT], g_ref[z, x, 1, :, lo : lo + UNIT]
            for k, value in enumerate((low[:, :CH], unfold(low[:, CH:], high[:, CH:]), high[:, :CH])):
                w_ref[pl.ds(pl.multiple_of(row + 16 * k, 16), 16), column : column + CH] = value


def lay_halves(g_ref, unit, w_ref):
    lo = unit * UNIT

    @pl.loop(0, NZ)
    def _(z):
        for pair in range(2):
            for c in range(2):
                row = z * 96 + pair * 48
                low = g_ref[z, 2 * pair, c, :, lo : lo + UNIT]
                high = g_ref[z, 2 * pair + 1, c, :, lo : lo + UNIT]
                for k, value in enumerate((low[:, :CH], unfold(low[:, CH:], high[:, CH:]), high[:, :CH])):
                    w_ref[pl.ds(pl.multiple_of(row + 16 * k, 16), 16), c * CH : (c + 1) * CH] = value


def norm_rows(values, gain):
    mean = jnp.mean(values, axis=-1, keepdims=True)
    centred = values - mean
    var = jnp.mean(centred * centred, axis=-1, keepdims=True)
    return centred * lax.rsqrt(var + 1e-05) * gain


def norm_into(src, gain, dst, first, end):
    @pl.loop(first, end)
    def _(i):
        rows = pl.ds(pl.multiple_of(i * 32, 32), 32)
        dst[rows, :] = norm_rows(src[rows, :].astype(F32), gain[...].reshape(1, D)).astype(BF16)


def times(x_ref, w_ref, column):
    return jnp.dot(
        x_ref[...], w_ref[:, pl.ds(pl.multiple_of(column, 256), 256)], preferred_element_type=F32
    )


def bounds(len_ref, place, bound_ref, member_ref, inverse_ref):
    lengths = len_ref[...].astype(F32)
    row = lax.broadcasted_iota(jnp.int32, (NREC, NREC), 0)
    col = lax.broadcasted_iota(jnp.int32, (NREC, NREC), 1)
    before = (row <= col).astype(BF16)
    wide = jnp.broadcast_to(lengths, (NREC, NREC))
    ends = jnp.dot(wide.astype(BF16), before, preferred_element_type=F32)
    first = (place.index * ROWS).astype(F32)
    t = lax.broadcasted_iota(jnp.int32, (ROWS, NREC), 0).astype(F32) + first
    end_row = jnp.broadcast_to(ends[:1], (ROWS, NREC))
    begin = jnp.max(jnp.where(end_row <= t, end_row, 0.0), axis=1, keepdims=True)
    finish = jnp.min(jnp.where(end_row > t, end_row, 65536.0), axis=1, keepdims=True)
    bound_ref[0] = jnp.broadcast_to(begin, (ROWS, NREC)) - t
    bound_ref[1] = jnp.broadcast_to(finish, (ROWS, NREC)) - t
    eye = row == col
    end_col = jnp.sum(jnp.where(eye, ends, 0.0), axis=1, keepdims=True)
    len_col = jnp.sum(jnp.where(eye, wide, 0.0), axis=1, keepdims=True)
    inverse_ref[...] = jnp.broadcast_to(1.0 / len_col, (NREC, NREC))
    at = lax.broadcasted_iota(jnp.int32, (NREC, ROWS), 1).astype(F32) + first
    inside = (at < end_col) & (at >= end_col - len_col)
    member_ref[...] = inside.astype(F32).astype(BF16)


def attend(i, q_ref, kv_ref, bound_ref, ctx_ref):
    factor = 1.4426950408889634 / HD**0.5
    span = 640

    top, lane0 = (i // 2) * 128, (i % 2) * 384
    rows = pl.ds(pl.multiple_of(top, 128), 128)
    window = pl.ds(pl.multiple_of(top, 128), span)
    offset = lax.broadcasted_iota(jnp.int32, (128, span), 1) - lax.broadcasted_iota(jnp.int32, (128, span), 0)
    offset = (offset - ROWS).astype(F32)
    inside = (offset >= bound_ref[0, rows, :1]) & (offset < bound_ref[1, rows, :1])
    bias = jnp.where(inside, 0.0, -1e30)
    outs = []
    for h in range(4):
        lo, hi = h * HD, (h + 1) * HD
        a, b = lo // 128 * 128, (hi + 127) // 128 * 128
        lane = lax.broadcasted_iota(jnp.int32, (128, b - a), 1) + a
        cols = pl.ds(pl.multiple_of(lane0 + a, 128), b - a)
        q = q_ref[rows, cols]
        q = jnp.where((lane >= lo) & (lane < hi), q.astype(F32), 0.0).astype(BF16)
        score = lax.dot_general(
            q, kv_ref[window, cols], (((1,), (1,)), ((), ())), preferred_element_type=F32
        )
        score = score + bias
        peak = jnp.max(score, axis=1, keepdims=True)
        expo = jnp.exp2((score - peak) * factor)
        total = jnp.sum(expo, axis=1, keepdims=True)
        values = kv_ref[window, pl.ds(pl.multiple_of(CH + lane0 + a, 128), b - a)]
        out = jnp.dot(expo.astype(BF16), values, preferred_element_type=F32)
        outs.append((a, out / total))
    for tile in range(3):
        lane = lax.broadcasted_iota(jnp.int32, (128, 128), 1)
        at = tile * 128
        one, two = outs[tile], outs[tile + 1]
        left = one[1][:, at - one[0] : at - one[0] + 128]
        right = two[1][:, at - two[0] : at - two[0] + 128]
        whole = jnp.where(lane < (tile + 1) * HD - at, left, right).astype(BF16)
        ctx_ref[rows, pl.ds(pl.multiple_of(lane0 + at, 128), 128)] = whole


def convolve(first, count, glu_ref, bound_ref, taps, gain, bias, act_ref):
    @pl.loop(0, count)
    def _(i):
        top = pl.multiple_of((i + first) * 32, 32)
        rows = pl.ds(top, 32)
        behind, ahead = bound_ref[0, rows, :], bound_ref[1, rows, :]
        for tile in range(CH // 128):
            lanes = slice(tile * 128, (tile + 1) * 128)
            depth = jnp.zeros((32, 128), F32)
            for j in range(KERNEL):
                source = glu_ref[tile, pl.ds(top + j + 1, 32), :]
                if j < HALF:
                    source = jnp.where(behind <= float(j - HALF), source, 0.0)
                elif j > HALF:
                    source = jnp.where(ahead > float(j - HALF), source, 0.0)
                depth = depth + taps[j : j + 1, lanes] * source
            moved = depth * gain[lanes].reshape(1, 128) + bias[lanes].reshape(1, 128)
            act_ref[rows, lanes] = (moved * jax.nn.sigmoid(moved)).astype(BF16)


def pool(copies, place, part_ref, give, take, sum_ref, sum16, rx, s2, rz, zb, xb, sb, out_ref):
    c = place.c
    copy = copies.send(give.at[1 - c], take, place.at(dc=1))
    copy.wait_recv()
    sum_ref[...] = part_ref[c] + take[...].astype(F32)
    sum16[...] = sum_ref[...].astype(BF16)
    got = []
    for k in range(1, NX):
        rows = pl.ds(pl.multiple_of((place.x + k) % NX * 32, 32), 32)
        got.append(copies.send(sum16.at[rows], rx.at[k - 1], place.at(dx=k)))
    total = sum_ref[pl.ds(pl.multiple_of(place.x * 32, 32), 32), :]
    for k, copy in enumerate(got):
        copy.wait_recv()
        total = total + rx[k].astype(F32)
    for j in range(NZ):
        s2[j] = total[8 * (j // 2) : 8 * (j // 2) + 8, 384 * (j % 2) : 384 * (j % 2) + 384]
    got = [copies.send(s2.at[(place.z + k) % NZ], rz.at[k - 1], place.at(dz=k)) for k in range(1, NZ)]
    total = s2[place.z]
    for k, copy in enumerate(got):
        copy.wait_recv()
        total = total + rz[k]
    zb[place.z] = total
    got = [copies.send(zb.at[place.z], zb.at[place.z], place.at(dz=k)) for k in range(1, NZ)]
    for copy in got:
        copy.wait_recv()
    parts = [jnp.concatenate([zb[2 * j], zb[2 * j + 1]], axis=1) for j in range(4)]
    xb[place.x] = jnp.concatenate(parts, axis=0).astype(BF16)
    got = [copies.send(xb.at[place.x], xb.at[place.x], place.at(dx=k)) for k in range(1, NX)]
    for copy in got:
        copy.wait_recv()
    copies.send(xb, sb, place.at(dc=1)).wait_recv()
    out_ref[c] = xb[...]
    out_ref[1 - c] = sb[...]


def block_kernel(
    h_frames, h_lengths, h_g_attn, h_wq, h_wk, h_wv, h_wo, h_g_conv, h_we, h_taps, h_bn_gain, h_bn_bias, h_ws, h_g_final,
    h_out, h_pooled,
    frames, lengths, g_attn, wq, wk, wv, wo, g_conv, we, taps, bn_gain, bn_bias, ws, g_final, out_ref, pooled_ref,
    g_ref, own_ref, w_kv, w_q, w_o, w_e, w_s, give, take, halo, normed, query, kv, ctx, after, glu16, glu_ref, rim, act,
    moved, bound_ref, member_ref, inverse_ref, part_ref, pool_give, pool_take, sum_ref, sum16, rx, s2, rz, zb, xb, sb,
    send_sem, recv_sem, load_sem,
):
    place = Place()
    barrier = pltpu.get_barrier_semaphore()
    partners = place.partners()
    for partner in partners:
        pl.semaphore_signal(barrier, inc=1, device_id=partner, device_id_type=MESH)
    pairs = (
        (h_wk, wk), (h_wv, wv), (h_wo, wo), (h_ws, ws), (h_frames, frames), (h_wq, wq), (h_we, we), (h_g_attn, g_attn),
        (h_lengths, lengths), (h_g_conv, g_conv), (h_taps, taps), (h_bn_gain, bn_gain), (h_bn_bias, bn_bias),
        (h_g_final, g_final),
    )
    loads = [pltpu.make_async_copy(src, dst, load_sem.at[k]) for k, (src, dst) in enumerate(pairs)]
    for load in loads:
        load.start()
    lead = place.c == 0
    for load in loads[:4]:
        load.wait()
    pack_own(own_ref, 0, wk[...].astype(F32), lead)
    pack_own(own_ref, 1, wv[...].astype(F32), lead)
    for k, ref in enumerate((wo, ws)):
        value = ref[...].astype(F32)
        theirs = jnp.where(lead, value[:, CH:], value[:, :CH])
        give[k] = jnp.concatenate([theirs, jnp.zeros((4, CH), F32)], axis=0).astype(BF16)
    for load in loads[4:]:
        load.wait()
    pl.semaphore_wait(barrier, len(partners))

    copies = Copies(send_sem, recv_sem)
    gather = Gather(copies, place, g_ref, own_ref)
    groups, sent = {}, {}

    def start(g):
        groups[g] = gather.start(g)
        if g == 0:
            sent["side"] = copies.send(give, take, place.at(dc=1))

    def pack_rest():
        pack_own(own_ref, 2, wq[...].astype(F32), lead)
        pack_own(own_ref, 4, we[:, :CH].astype(F32), lead)
        pack_own(own_ref, 5, we[:, CH:].astype(F32), lead)

    def pack_halves():
        sent["side"].wait_recv()
        for k, (unit, ref) in enumerate(((3, wo), (6, ws))):
            value = ref[...].astype(F32)
            own = jnp.where(lead, value[:, :CH], value[:, CH:])
            got = take[k].astype(F32)[:12]
            both = jnp.where(lead, jnp.concatenate([own, got], axis=0), jnp.concatenate([got, own], axis=0))
            pack_own(own_ref, unit, both, place.x % 2 == 0)

    def arrived(unit):
        for g, (first, end, _, _) in enumerate(GROUPS):
            if first <= unit < end:
                assert groups[g].finish()

    def lay_kv():
        arrived(0)
        lay_rows(g_ref, 0, w_kv, 0)
        lay_rows(g_ref, 1, w_kv, CH)

    far = pl.ds(pl.multiple_of(place.c * (2 * ROWS), ROWS), ROWS)

    def send_frames():
        sent["frames"] = copies.send(frames, halo, place.beside(2 * place.c - 1))

    def norm_halo(first, end):
        if first == 0:
            sent["frames"].wait_recv()
        norm_into(halo, g_attn, normed.at[pl.ds(ROWS, ROWS)], first, end)

    def make_kv(half):
        @pl.loop(half * 3, half * 3 + 3)
        def _(n):
            cols = pl.ds(pl.multiple_of(n * 256, 256), 256)
            both = times(normed, w_kv, n * 256).astype(BF16)
            kv[ROWS : 2 * ROWS, cols] = both[:ROWS]
            kv[far, cols] = both[ROWS:]

    def send_kv():
        sent["kv"] = copies.send(kv.at[pl.ds(ROWS, ROWS)], kv.at[far], place.at(dc=1))

    def lay_q():
        arrived(2)
        lay_rows(g_ref, 2, w_q, 0)

    def make_q():
        @pl.loop(0, 3)
        def _(n):
            query[:, pl.ds(pl.multiple_of(n * 256, 256), 256)] = times(normed.at[pl.ds(0, ROWS)], w_q, n * 256).astype(BF16)

    def lay_o():
        arrived(3)
        lay_halves(g_ref, 3, w_o)

    def attention(k):
        if k == 0:
            sent["kv"].wait_recv()
        attend(k, query, kv, bound_ref, ctx)

    def make_after():
        @pl.loop(0, 6)
        def _(n):
            cols = pl.ds(pl.multiple_of(n * 256, 256), 256)
            after[:, cols] = (frames[:, cols].astype(F32) + times(ctx, w_o, n * 256)).astype(BF16)

    def lay_e():
        arrived(4)
        lay_rows(g_ref, 4, w_e, 0)
        lay_rows(g_ref, 5, w_e, CH)

    def make_glu(n):
        gate = times(normed.at[pl.ds(0, ROWS)], w_e, CH + n * 256)
        value = times(normed.at[pl.ds(0, ROWS)], w_e, n * 256)
        glu = (value * jax.nn.sigmoid(gate)).astype(BF16)
        glu16[:, n * 256 : n * 256 + 256] = glu
        wide = glu.astype(F32)
        glu_ref[2 * n, 16 : 16 + ROWS, :] = wide[:, :128]
        glu_ref[2 * n + 1, 16 : 16 + ROWS, :] = wide[:, 128:]

    def send_rim():
        sent["rim0"] = copies.send(glu16.at[pl.ds(0, 16)], rim.at[1], place.beside(-1))
        sent["rim1"] = copies.send(glu16.at[pl.ds(ROWS - 16, 16)], rim.at[0], place.beside(1))

    def conv(first, count):
        convolve(first, count, glu_ref, bound_ref, taps, bn_gain, bn_bias, act)

    def conv_edges():
        sent["rim0"].wait_recv()
        sent["rim1"].wait_recv()
        for tile in range(CH // 128):
            lanes = slice(tile * 128, (tile + 1) * 128)
            glu_ref[tile, :16, :] = rim[0, :, lanes].astype(F32)
            glu_ref[tile, 16 + ROWS :, :] = rim[1, :, lanes].astype(F32)
        conv(0, 1)
        conv(7, 1)

    def lay_s():
        arrived(6)
        lay_halves(g_ref, 6, w_s)

    def make_moved():
        @pl.loop(0, 6)
        def _(n):
            cols = pl.ds(pl.multiple_of(n * 256, 256), 256)
            moved[:, cols] = after[:, cols].astype(F32) + times(act, w_s, n * 256)

    def finish():
        norm_into(moved, g_final, out_ref, 0, 8)
        sent["out"] = pltpu.make_async_copy(out_ref, h_out, load_sem.at[len(pairs)])
        sent["out"].start()
        for h in range(2):
            for n in range(3):
                cols = slice(h * CH + n * 256, h * CH + n * 256 + 256)
                sums = jnp.dot(member_ref[...], out_ref[:, cols], preferred_element_type=F32) * inverse_ref[:, :1]
                part_ref[h, :, n * 256 : n * 256 + 256] = sums
                pool_give[h, :, n * 256 : n * 256 + 256] = sums.astype(BF16)

    tasks = {
        "packrest": pack_rest,
        "packos": pack_halves,
        "bounds": lambda: bounds(lengths, place, bound_ref, member_ref, inverse_ref),
        "norma": lambda: norm_into(frames, g_attn, normed, 0, 4),
        "normb": lambda: norm_into(frames, g_attn, normed, 4, 8),
        "sendfr": send_frames,
        "normx": lambda: norm_halo(0, 4),
        "normy": lambda: norm_halo(4, 8),
        "laykv": lay_kv,
        "mmkv0": lambda: make_kv(0),
        "mmkv1": lambda: make_kv(1),
        "sendkv": send_kv,
        "layq": lay_q,
        "mmq": make_q,
        "layo": lay_o,
        "att0": lambda: attention(0),
        "att1": lambda: attention(1),
        "att2": lambda: attention(2),
        "att3": lambda: attention(3),
        "mmo": make_after,
        "normc": lambda: norm_into(after, g_conv, normed, 0, 4),
        "normd": lambda: norm_into(after, g_conv, normed, 4, 8),
        "laye": lay_e,
        "mme0": lambda: make_glu(0),
        "mme1": lambda: make_glu(1),
        "mme2": lambda: make_glu(2),
        "sendrim": send_rim,
        "conv0": lambda: conv(1, 3),
        "conv1": lambda: conv(4, 3),
        "lays": lay_s,
        "conv2": conv_edges,
        "mms": make_moved,
        "fin": finish,
    }
    for name in PLAN:
        if name.startswith("start"):
            start(int(name[5:]))
        elif name[0].isdigit():
            groups[int(name[0])].step(int(name[1]))
        else:
            tasks[name]()
    pool(copies, place, part_ref, pool_give, pool_take, sum_ref, sum16, rx, s2, rz, zb, xb, sb, pooled_ref)
    last = pltpu.make_async_copy(pooled_ref, h_pooled, load_sem.at[len(pairs) + 1])
    last.start()
    copies.finish()
    sent["out"].wait()
    last.wait()


def local(frames, lengths, norm_attn, w_query, w_key, w_value, w_out, norm_conv, w_expand, kernel, bn_gain,
          bn_bias, w_shrink, norm_final):
    hbm = pl.BlockSpec(memory_space=pl.ANY)
    block_out, halves = pl.pallas_call(
        block_kernel,
        out_shape=[
            jax.ShapeDtypeStruct((ROWS, D), BF16),
            jax.ShapeDtypeStruct((2, NX, 32, CH), BF16),
        ],
        in_specs=[hbm] * 14,
        out_specs=[hbm] * 2,
        scratch_shapes=[
            pltpu.VMEM((ROWS, D), BF16),
            pltpu.VMEM((1, NREC), jnp.int32),
            pltpu.VMEM((D,), F32),
            pltpu.VMEM((24, CH), BF16),
            pltpu.VMEM((24, CH), BF16),
            pltpu.VMEM((24, CH), BF16),
            pltpu.VMEM((12, D), BF16),
            pltpu.VMEM((D,), F32),
            pltpu.VMEM((24, D), BF16),
            pltpu.VMEM((KERNEL, CH), F32),
            pltpu.VMEM((CH,), F32),
            pltpu.VMEM((CH,), F32),
            pltpu.VMEM((12, D), BF16),
            pltpu.VMEM((D,), F32),
            pltpu.VMEM((ROWS, D), BF16),
            pltpu.VMEM((2, NX, 32, CH), BF16),
            pltpu.VMEM((NZ, NX, 2, 16, COLS), BF16),
            pltpu.VMEM((16, COLS), BF16),
            pltpu.VMEM((D, 2 * CH), BF16),
            pltpu.VMEM((D, CH), BF16),
            pltpu.VMEM((CH, D), BF16),
            pltpu.VMEM((D, 2 * CH), BF16),
            pltpu.VMEM((CH, D), BF16),
            pltpu.VMEM((2, 16, CH), BF16),
            pltpu.VMEM((2, 16, CH), BF16),
            pltpu.VMEM((ROWS, D), BF16),
            pltpu.VMEM((2 * ROWS, D), BF16),
            pltpu.VMEM((ROWS, CH), BF16),
            pltpu.VMEM((3 * ROWS, 2 * CH), BF16),
            pltpu.VMEM((ROWS, CH), BF16),
            pltpu.VMEM((ROWS, D), BF16),
            pltpu.VMEM((ROWS, CH), BF16),
            pltpu.VMEM((CH // 128, ROWS + 32, 128), F32),
            pltpu.VMEM((2, 16, CH), BF16),
            pltpu.VMEM((ROWS, CH), BF16),
            pltpu.VMEM((ROWS, D), F32),
            pltpu.VMEM((2, ROWS, NREC), F32),
            pltpu.VMEM((NREC, ROWS), BF16),
            pltpu.VMEM((NREC, NREC), F32),
            pltpu.VMEM((2, NREC, CH), F32),
            pltpu.VMEM((2, NREC, CH), BF16),
            pltpu.VMEM((NREC, CH), BF16),
            pltpu.VMEM((NREC, CH), F32),
            pltpu.VMEM((NREC, CH), BF16),
            pltpu.VMEM((NX - 1, 32, CH), BF16),
            pltpu.VMEM((NZ, 8, 384), F32),
            pltpu.VMEM((NZ - 1, 8, 384), F32),
            pltpu.VMEM((NZ, 8, 384), F32),
            pltpu.VMEM((NX, 32, CH), BF16),
            pltpu.VMEM((NX, 32, CH), BF16),
            pltpu.SemaphoreType.DMA((N_COPIES,)),
            pltpu.SemaphoreType.DMA((N_COPIES,)),
            pltpu.SemaphoreType.DMA((16,)),
        ],
        compiler_params=pltpu.CompilerParams(
            collective_id=0, has_side_effects=True, vmem_limit_bytes=60 << 20
        ),
        cost_estimate=pl.CostEstimate(flops=5_000_000_000, bytes_accessed=20_000_000, transcendentals=3_000_000),
    )(
        frames, lengths.reshape(1, NREC), norm_attn, w_query, w_key, w_value, w_out,
        norm_conv, w_expand, kernel, bn_gain, bn_bias, w_shrink,
        norm_final,
    )
    halves = halves.reshape(2, NREC, CH).astype(F32)
    return block_out, jnp.concatenate([halves[0], halves[1]], axis=1)


def solution(mesh):
    return jax.shard_map(
        local,
        mesh=mesh,
        in_specs=(
            P(("rep", "seq"), None),
            P("rep"),
            P(),
            P("seq", None),
            P("seq", None),
            P("seq", None),
            P("seq", None),
            P(),
            P("seq", None),
            P(),
            P(),
            P(),
            P("seq", None),
            P(),
        ),
        out_specs=(P(("rep", "seq"), None), P("rep", None)),
        check_vma=False,
    )
```

profile of v0, /device:TPU:1, one launch (start us, length us, event | category | flops | bytes accessed | tf_op | source)
XLA Modules:
  0.0 107.6 jit_solution(18341590194902533749)
XLA Ops:
  0.6 103.6 %shard_map.149 = (bf16[256,1536]{1,0:T(8,128)(2,1)}, bf16[2,4,32,768]{3,2,1,0:T(8,128)(2,1)}) custom-call(bf16[256,1536]{1,0:T(8,128)(2,1)} %h_frames.1, s32[1,128]{1,0:T(1,128)} %bitcast.5, f32[1536]{0:T(1024)} %h_g_attn.1, bf16[24,768]{1,0:T(8,128)(2,1)} %h_wq.1, bf16[24,768]{1,0:T(8,128)(2,1)} %h_wk.1, bf16[24,768]{1,0:T(8,128)(2,1)} %h_wv.1, ...), custom_call_target="tpu_custom_call" | custom-call | flops 5000000000 | bytes 20000000 | tf_op jit(solution)/shard_map/pallas_call | solution.py:658
  104.2 1.1 %fusion = (f32[1,4,32,768]{3,2,1,0:T(8,128)S(1)}, f32[1,4,32,768]{3,2,1,0:T(8,128)S(1)}) fusion(bf16[2,4,32,768]{3,2,1,0:T(8,128)(2,1)} %get-tuple-element.5), kind=kLoop, calls=%fused_computation.1 | loop fusion | bytes 1572864 | tf_op jit(solution)/shard_map/slice | solution.py:731
  105.3 0.0 copy-start
  105.3 1.0 pad_maximum_fusion
  106.3 0.4 copy-done
  106.7 0.9 copy.17
Async XLA Ops:
  105.3 1.4 %copy-start = (bf16[256,1536]{1,0:T(8,128)(2,1)S(1)}, bf16[256,1536]{1,0:T(8,128)(2,1)}, u32[]{:S(2)}) copy-start(bf16[256,1536]{1,0:T(8,128)(2,1)} %get-tuple-element.10) | copy-start | bytes 2359300
where the time goes:
time: 108 us
  Pallas kernels  104 us (96%)
  local copies, waits for them, and re-layouts  2.41 us (2%)
    pallas_call x1, Pallas kernels, local(): pl.pallas_call(block_kernel, out_shape=[jax.ShapeDtypeStruct((ROWS, D), B...  104 us

commit v1 on v0

--- a/solution.py
+++ b/solution.py
@@ -25,7 +25,7 @@
     (4, 6, (5, 5, 8), ('ring', 'ring', 'ring', 'ring', 'straight')),
     (6, 7, (1, 0, 8), ('straight', 'ring', 'hops', 'ring', 'ring')),
 )
-N_COPIES = 112
+N_COPIES = 71
 PLAN = (
     "start0", "sendfr", "packrest", "bounds", "packos", "01", "start1", "00", "02", "start3", "norma",
     "normb", "01", "11", "12", "start2", "00", "32", "01", "11", "12", "21", "normx", "normy", "10", "22",
@@ -409,33 +409,43 @@
     copy.wait_recv()
     sum_ref[...] = part_ref[c] + take[...].astype(F32)
     sum16[...] = sum_ref[...].astype(BF16)
-    got = []
-    for k in range(1, NX):
-        rows = pl.ds(pl.multiple_of((place.x + k) % NX * 32, 32), 32)
-        got.append(copies.send(sum16.at[rows], rx.at[k - 1], place.at(dx=k)))
+    def exchange(axis, n, src, dst, size):
+        sems = copies.sems()
+
+        def make(src, dst, device):
+            return pltpu.make_async_remote_copy(
+                src_ref=src, dst_ref=dst, device_id=device, device_id_type=MESH, **sems
+            )
+
+        for k in range(1, n):
+            make(src(k), dst(k), place.at(**{"d" + axis: k})).start()
+        total = make(size, size, place.at(dc=1))
+        copies.all.append(total)
+        total.wait_recv()
+
+    def mine(k):
+        return sum16.at[pl.ds(pl.multiple_of((place.x + k) % NX * 32, 32), 32)]
+
+    exchange("x", NX, mine, lambda k: rx.at[k - 1], rx)
     total = sum_ref[pl.ds(pl.multiple_of(place.x * 32, 32), 32), :]
-    for k, copy in enumerate(got):
-        copy.wait_recv()
+    for k in range(NX - 1):
         total = total + rx[k].astype(F32)
     for j in range(NZ):
         s2[j] = total[8 * (j // 2) : 8 * (j // 2) + 8, 384 * (j % 2) : 384 * (j % 2) + 384]
-    got = [copies.send(s2.at[(place.z + k) % NZ], rz.at[k - 1], place.at(dz=k)) for k in range(1, NZ)]
+    exchange("z", NZ, lambda k: s2.at[(place.z + k) % NZ], lambda k: rz.at[k - 1], rz)
     total = s2[place.z]
-    for k, copy in enumerate(got):
-        copy.wait_recv()
+    for k in range(NZ - 1):
         total = total + rz[k]
     zb[place.z] = total
-    got = [copies.send(zb.at[place.z], zb.at[place.z], place.at(dz=k)) for k in range(1, NZ)]
-    for copy in got:
-        copy.wait_recv()
+    exchange("z", NZ, lambda k: zb.at[place.z], lambda k: zb.at[place.z], rz)
     parts = [jnp.concatenate([zb[2 * j], zb[2 * j + 1]], axis=1) for j in range(4)]
     xb[place.x] = jnp.concatenate(parts, axis=0).astype(BF16)
-    got = [copies.send(xb.at[place.x], xb.at[place.x], place.at(dx=k)) for k in range(1, NX)]
-    for copy in got:
-        copy.wait_recv()
+    exchange("x", NX, lambda k: xb.at[place.x], lambda k: xb.at[place.x], rx)
     copies.send(xb, sb, place.at(dc=1)).wait_recv()
-    out_ref[c] = xb[...]
-    out_ref[1 - c] = sb[...]
+    for k in range(NX):
+        rows = slice(32 * k, 32 * k + 32)
+        out_ref[rows, pl.ds(pl.multiple_of(c * CH, CH), CH)] = xb[k]
+        out_ref[rows, pl.ds(pl.multiple_of((1 - c) * CH, CH), CH)] = sb[k]
 
 
 def block_kernel(
@@ -655,11 +665,11 @@
 def local(frames, lengths, norm_attn, w_query, w_key, w_value, w_out, norm_conv, w_expand, kernel, bn_gain,
           bn_bias, w_shrink, norm_final):
     hbm = pl.BlockSpec(memory_space=pl.ANY)
-    block_out, halves = pl.pallas_call(
+    block_out, pooled = pl.pallas_call(
         block_kernel,
         out_shape=[
             jax.ShapeDtypeStruct((ROWS, D), BF16),
-            jax.ShapeDtypeStruct((2, NX, 32, CH), BF16),
+            jax.ShapeDtypeStruct((NREC, D), BF16),
         ],
         in_specs=[hbm] * 14,
         out_specs=[hbm] * 2,
@@ -679,7 +689,7 @@
             pltpu.VMEM((12, D), BF16),
             pltpu.VMEM((D,), F32),
             pltpu.VMEM((ROWS, D), BF16),
-            pltpu.VMEM((2, NX, 32, CH), BF16),
+            pltpu.VMEM((NREC, D), BF16),
             pltpu.VMEM((NZ, NX, 2, 16, COLS), BF16),
             pltpu.VMEM((16, COLS), BF16),
             pltpu.VMEM((D, 2 * CH), BF16),
@@ -727,8 +737,7 @@
         norm_conv, w_expand, kernel, bn_gain, bn_bias, w_shrink,
         norm_final,
     )
-    halves = halves.reshape(2, NREC, CH).astype(F32)
-    return block_out, jnp.concatenate([halves[0], halves[1]], axis=1)
+    return block_out, pooled.astype(F32)
 
 
 def solution(mesh):

time: 108 us -> 107 us (level)
  local copies, waits for them, and re-layouts: 2.41 us -> 0.88 us
    convert_element_type x0 -> x1, other arithmetic: none -> 2.03 us  [local(): return (block_out, pooled.astype(F32))]
    slice x1 -> x0, local copies, waits for them, and re-layouts: 1.08 us -> none  [local(): return (block_out, jnp.concatenate([halves[0], halves[1]], axis=1))]
where the time goes in v1:
time: 107 us; the launch traced here: 106 us
  Pallas kernels  103 us (96%)
  other arithmetic  2.03 us (2%)
    pallas_call x1, Pallas kernels, local(): pl.pallas_call(block_kernel, out_shape=[jax.ShapeDtypeStruct((ROWS, D), B...  103 us

profile of v1, /device:TPU:1, one launch (start us, length us, event | category | flops | bytes accessed | tf_op | source)
XLA Modules:
  0.0 106.4 jit_solution(17581519988111682538)
XLA Ops:
  0.6 102.9 %shard_map.149 = (bf16[256,1536]{1,0:T(8,128)(2,1)}, bf16[128,1536]{1,0:T(8,128)(2,1)}) custom-call(bf16[256,1536]{1,0:T(8,128)(2,1)} %h_frames.1, s32[1,128]{1,0:T(1,128)} %bitcast.1, f32[1536]{0:T(1024)} %h_g_attn.1, bf16[24,768]{1,0:T(8,128)(2,1)} %h_wq.1, bf16[24,768]{1,0:T(8,128)(2,1)} %h_wk.1, bf16[24,768]{1,0:T(8,128)(2,1)} %h_wv.1, ...), custom_call_target="tpu_custom_call" | custom-call | flops 5000000000 | bytes 20000000 | tf_op jit(solution)/shard_map/pallas_call | solution.py:668
  103.5 0.0 copy-start
  103.5 2.0 %convert_element_type.3 = f32[128,1536]{1,0:T(8,128)} convert(bf16[128,1536]{1,0:T(8,128)(2,1)} %get-tuple-element.5) | non-fusion elementwise | flops 196608 | bytes 1179648 | tf_op jit(solution)/shard_map/convert_element_type | solution.py:740
  105.6 0.0 copy-done
  105.6 0.9 copy.17
Async XLA Ops:
  103.5 2.0 %copy-start = (bf16[256,1536]{1,0:T(8,128)(2,1)S(1)}, bf16[256,1536]{1,0:T(8,128)(2,1)}, u32[]{:S(2)}) copy-start(bf16[256,1536]{1,0:T(8,128)(2,1)} %get-tuple-element.8) | copy-start | bytes 2359300

commit v2 on v1

--- a/solution.py
+++ b/solution.py
@@ -25,7 +25,7 @@
     (4, 6, (5, 5, 8), ('ring', 'ring', 'ring', 'ring', 'straight')),
     (6, 7, (1, 0, 8), ('straight', 'ring', 'hops', 'ring', 'ring')),
 )
-N_COPIES = 71
+N_COPIES = 83
 PLAN = (
     "start0", "sendfr", "packrest", "bounds", "packos", "01", "start1", "00", "02", "start3", "norma",
     "normb", "01", "11", "12", "start2", "00", "32", "01", "11", "12", "21", "normx", "normy", "10", "22",
@@ -405,10 +405,7 @@
 
 def pool(copies, place, part_ref, give, take, sum_ref, sum16, rx, s2, rz, zb, xb, sb, out_ref):
     c = place.c
-    copy = copies.send(give.at[1 - c], take, place.at(dc=1))
-    copy.wait_recv()
-    sum_ref[...] = part_ref[c] + take[...].astype(F32)
-    sum16[...] = sum_ref[...].astype(BF16)
+
     def exchange(axis, n, src, dst, size):
         sems = copies.sems()
 
@@ -421,31 +418,54 @@
             make(src(k), dst(k), place.at(**{"d" + axis: k})).start()
         total = make(size, size, place.at(dc=1))
         copies.all.append(total)
-        total.wait_recv()
-
-    def mine(k):
-        return sum16.at[pl.ds(pl.multiple_of((place.x + k) % NX * 32, 32), 32)]
-
-    exchange("x", NX, mine, lambda k: rx.at[k - 1], rx)
-    total = sum_ref[pl.ds(pl.multiple_of(place.x * 32, 32), 32), :]
-    for k in range(NX - 1):
-        total = total + rx[k].astype(F32)
-    for j in range(NZ):
-        s2[j] = total[8 * (j // 2) : 8 * (j // 2) + 8, 384 * (j % 2) : 384 * (j % 2) + 384]
-    exchange("z", NZ, lambda k: s2.at[(place.z + k) % NZ], lambda k: rz.at[k - 1], rz)
-    total = s2[place.z]
-    for k in range(NZ - 1):
-        total = total + rz[k]
-    zb[place.z] = total
-    exchange("z", NZ, lambda k: zb.at[place.z], lambda k: zb.at[place.z], rz)
-    parts = [jnp.concatenate([zb[2 * j], zb[2 * j + 1]], axis=1) for j in range(4)]
-    xb[place.x] = jnp.concatenate(parts, axis=0).astype(BF16)
-    exchange("x", NX, lambda k: xb.at[place.x], lambda k: xb.at[place.x], rx)
-    copies.send(xb, sb, place.at(dc=1)).wait_recv()
-    for k in range(NX):
-        rows = slice(32 * k, 32 * k + 32)
-        out_ref[rows, pl.ds(pl.multiple_of(c * CH, CH), CH)] = xb[k]
-        out_ref[rows, pl.ds(pl.multiple_of((1 - c) * CH, CH), CH)] = sb[k]
+        return total
+
+    def third(n):
+        cols = slice(n * 256, (n + 1) * 256)
+        span = pl.ds(n * 256, 256)
+        copy = copies.send(give.at[1 - c, :, span], take.at[:, span], place.at(dc=1))
+        yield
+        copy.wait_recv()
+        sum_ref[:, cols] = part_ref[c, :, cols] + take[:, cols].astype(F32)
+        sum16[:, cols] = sum_ref[:, cols].astype(BF16)
+
+        def theirs(k):
+            return sum16.at[pl.ds(pl.multiple_of((place.x + k) % NX * 32, 32), 32), span]
+
+        copy = exchange("x", NX, theirs, lambda k: rx.at[n, k - 1], rx.at[n])
+        yield
+        copy.wait_recv()
+        total = sum_ref[pl.ds(pl.multiple_of(place.x * 32, 32), 32), cols]
+        for k in range(NX - 1):
+            total = total + rx[n, k].astype(F32)
+        for j in range(NZ):
+            s2[n, j] = total[8 * (j // 2) : 8 * (j // 2) + 8, 128 * (j % 2) : 128 * (j % 2) + 128]
+        copy = exchange("z", NZ, lambda k: s2.at[n, (place.z + k) % NZ], lambda k: rz.at[n, k - 1], rz.at[n])
+        yield
+        copy.wait_recv()
+        total = s2[n, place.z]
+        for k in range(NZ - 1):
+            total = total + rz[n, k]
+        zb[n, place.z] = total
+        copy = exchange("z", NZ, lambda k: zb.at[n, place.z], lambda k: zb.at[n, place.z], rz.at[n])
+        yield
+        copy.wait_recv()
+        parts = [jnp.concatenate([zb[n, 2 * j], zb[n, 2 * j + 1]], axis=1) for j in range(4)]
+        xb[n, place.x] = jnp.concatenate(parts, axis=0).astype(BF16)
+        copy = exchange("x", NX, lambda k: xb.at[n, place.x], lambda k: xb.at[n, place.x], rx.at[n])
+        yield
+        copy.wait_recv()
+        copy = copies.send(xb.at[n], sb.at[n], place.at(dc=1))
+        yield
+        copy.wait_recv()
+        for k in range(NX):
+            rows = slice(32 * k, 32 * k + 32)
+            out_ref[rows, pl.ds(pl.multiple_of(c * CH + n * 256, 256), 256)] = xb[n, k]
+            out_ref[rows, pl.ds(pl.multiple_of((1 - c) * CH + n * 256, 256), 256)] = sb[n, k]
+
+    live = [third(n) for n in range(3)]
+    while live:
+        live = [one for one in live if next(one, True) is None]
 
 
 def block_kernel(
@@ -718,12 +738,12 @@
             pltpu.VMEM((NREC, CH), BF16),
             pltpu.VMEM((NREC, CH), F32),
             pltpu.VMEM((NREC, CH), BF16),
-            pltpu.VMEM((NX - 1, 32, CH), BF16),
-            pltpu.VMEM((NZ, 8, 384), F32),
-            pltpu.VMEM((NZ - 1, 8, 384), F32),
-            pltpu.VMEM((NZ, 8, 384), F32),
-            pltpu.VMEM((NX, 32, CH), BF16),
-            pltpu.VMEM((NX, 32, CH), BF16),
+            pltpu.VMEM((3, NX - 1, 32, 256), BF16),
+            pltpu.VMEM((3, NZ, 8, 128), F32),
+            pltpu.VMEM((3, NZ - 1, 8, 128), F32),
+            pltpu.VMEM((3, NZ, 8, 128), F32),
+            pltpu.VMEM((3, NX, 32, 256), BF16),
+            pltpu.VMEM((3, NX, 32, 256), BF16),
             pltpu.SemaphoreType.DMA((N_COPIES,)),
             pltpu.SemaphoreType.DMA((N_COPIES,)),
             pltpu.SemaphoreType.DMA((16,)),

time: 107 us -> 105 us (0.981)
  Pallas kernels: 103 us -> 101 us
    pallas_call x1, Pallas kernels: 103 us -> 101 us  [local(): pl.pallas_call(block_kernel, out_shape=[jax.ShapeDtypeStruct((ROWS, D), B...]
where the time goes in v2:
time: 105 us
  Pallas kernels  101 us (96%)
  other arithmetic  2.03 us (2%)
    pallas_call x1, Pallas kernels, local(): pl.pallas_call(block_kernel, out_shape=[jax.ShapeDtypeStruct((ROWS, D), B...  101 us

profile of v2, /device:TPU:1, one launch (start us, length us, event | category | flops | bytes accessed | tf_op | source)
XLA Modules:
  0.0 105.0 jit_solution(10683361222748187272)
XLA Ops:
  0.6 101.5 %shard_map.149 = (bf16[256,1536]{1,0:T(8,128)(2,1)}, bf16[128,1536]{1,0:T(8,128)(2,1)}) custom-call(bf16[256,1536]{1,0:T(8,128)(2,1)} %h_frames.1, s32[1,128]{1,0:T(1,128)} %bitcast.1, f32[1536]{0:T(1024)} %h_g_attn.1, bf16[24,768]{1,0:T(8,128)(2,1)} %h_wq.1, bf16[24,768]{1,0:T(8,128)(2,1)} %h_wk.1, bf16[24,768]{1,0:T(8,128)(2,1)} %h_wv.1, ...), custom_call_target="tpu_custom_call" | custom-call | flops 5000000000 | bytes 20000000 | tf_op jit(solution)/shard_map/pallas_call | solution.py:688
  102.1 0.0 copy-start
  102.1 2.0 %convert_element_type.3 = f32[128,1536]{1,0:T(8,128)} convert(bf16[128,1536]{1,0:T(8,128)(2,1)} %get-tuple-element.5) | non-fusion elementwise | flops 196608 | bytes 1179648 | tf_op jit(solution)/shard_map/convert_element_type | solution.py:760
  104.2 0.0 copy-done
  104.2 0.9 copy.17
Async XLA Ops:
  102.1 2.0 %copy-start = (bf16[256,1536]{1,0:T(8,128)(2,1)S(1)}, bf16[256,1536]{1,0:T(8,128)(2,1)}, u32[]{:S(2)}) copy-start(bf16[256,1536]{1,0:T(8,128)(2,1)} %get-tuple-element.8) | copy-start | bytes 2359300
